TPU v7x, 128 devices: a whole 4x4x4 slice. The times are simulated.
128 devices in a mesh: fsdp: 8 (over z, core), tp: 16 (over y, x).
Axes of the slice: x: 4, y: 4, z: 4, core: 2. Of those that a mesh axis runs over, the one named last changes fastest.
Arguments:
- base_projection: bfloat16 [2, 16384, 18432], P(None, ('fsdp', 'tp')), may hold values from -6 to 6
- down_factor_transposed: bfloat16 [2, 64, 16384], P(None, None, ('fsdp', 'tp')), may hold values from -2 to 2
- up_factor: bfloat16 [2, 64, 18432], P(None, 'fsdp'), may hold values from -6 to 6
- block_permutation: int32 [144], replicated, may hold values from 0 to 143, each once
Outputs:
- merged: bfloat16 [2, 16384, 18432], P(None, 'fsdp', 'tp')
Inputs may be any that keep to these rules, and one draw needn't show every extreme that they name: `block_permutation`: each block index appears exactly once.
All inputs are finite; a program needn't handle non-finite values.
Results may differ from a plain program's by a relative error of at most 0.001.
Values may be sent and summed in bfloat16 or wider, within the bound.
No kernel may reach another device: no remote copies, remote signals or barrier semaphores. Data moves between devices by JAX's collectives and lax.ppermute only.
A program may use at most 128 MiB of HBM per device.

v0:
```python
import jax
import jax.numpy as jnp
from jax import lax
from jax.sharding import PartitionSpec as P

BLOCK = 128


update_scale = 2.0


def permute_columns(values, order):
    lead = values.shape[:-1]
    blocks = values.reshape(lead + (values.shape[-1] // BLOCK, BLOCK))
    blocks = jnp.take(blocks, order, axis=-2)
    return blocks.reshape(lead + (order.shape[0] * BLOCK,))


def combine(base_slice, factor_rows, factor_cols):
    update_product = jnp.dot(factor_rows.T, factor_cols, preferred_element_type=jnp.float32)
    return (base_slice.astype(jnp.float32) + update_scale * update_product).astype(jnp.bfloat16)


def per_device(base_projection, down_factor_transposed, up_factor, block_permutation):
    servers = lax.axis_size("tp")
    per_server = block_permutation.shape[0] // servers
    local_blocks = lax.dynamic_slice_in_dim(
        block_permutation, lax.axis_index("tp") * per_server, per_server
    )
    layers = base_projection.shape[0]
    merged_outputs = []
    local_down_factor = lax.all_gather(down_factor_transposed, "tp", axis=2, tiled=True)
    local_up_factor = permute_columns(
        lax.all_gather(up_factor, "fsdp", axis=1, tiled=True), local_blocks
    )
    for layer_index in range(layers):
        ordered = permute_columns(base_projection[layer_index], block_permutation)
        received = lax.all_to_all(ordered, "tp", split_axis=1, concat_axis=0, tiled=True)
        merged_outputs.append(
            combine(received, local_down_factor[layer_index], local_up_factor[layer_index])
        )
    return jnp.stack(merged_outputs)


def solution(mesh):
    return jax.shard_map(
        per_device,
        mesh=mesh,
        in_specs=(
            P(None, ("fsdp", "tp"), None),
            P(None, None, ("fsdp", "tp")),
            P(None, "fsdp", None),
            P(),
        ),
        out_specs=P(None, "fsdp", "tp"),
        check_vma=False,
    )
```

profile of v0, /device:TPU:0, one launch (start us, length us, event | category | flops | bytes accessed | tf_op | source)
XLA Modules:
  0.0 294.6 jit_solution(10080958054724903758)
XLA Ops:
  6.5 0.0 all-gather.2.cloned.1.call-start
  6.5 0.7 all-gather.2.cloned.1.call-update
  7.3 0.7 compare_and_fusion
  7.9 0.7 compare_select_fusion
  8.6 8.5 %fusion.8 = (bf16[1,128,18432]{2,1,0:T(8,128)(2,1)}, bf16[1,128,18432]{2,1,0:T(8,128)(2,1)}) fusion(bf16[2,128,18432]{2,1,0:T(8,128)(2,1)} %param.6), kind=kLoop, calls=%fused_computation.30 | loop fusion | bytes 18874368 | tf_op jit(solution)/shard_map/slice | solution.py:37
  17.1 6.6 %copy.25 = bf16[1,128,18432]{1,2,0:T(8,128)(2,1)} copy(bf16[1,128,18432]{2,1,0:T(8,128)(2,1)} %get-tuple-element.8) | data formatting | bytes 9437184
  23.8 6.6 %copy.14 = bf16[128,144,128]{2,0,1:T(8,128)(2,1)} copy(bf16[128,144,128]{0,2,1:T(8,128)(2,1)} %bitcast.65) | data formatting | bytes 9437184 | tf_op jit(solution)/shard_map/reshape;squeeze | solution.py:14
  30.4 6.6 %copy.26 = bf16[1,128,18432]{1,2,0:T(8,128)(2,1)} copy(bf16[1,128,18432]{2,1,0:T(8,128)(2,1)} %get-tuple-element.9) | data formatting | bytes 9437184
  37.0 6.8 %copy.20 = bf16[128,144,128]{2,0,1:T(8,128)(2,1)} copy(bf16[128,144,128]{0,2,1:T(8,128)(2,1)} %bitcast.66) | data formatting | bytes 9437184 | tf_op jit(solution)/shard_map/reshape;squeeze | solution.py:14
  43.8 10.0 %gather_fusion.1 = bf16[144,128,128]{2,1,0:T(8,128)(2,1)} fusion(bf16[128,144,128]{2,0,1:T(8,128)(2,1)} %copy.14, s32[1024]{0:T(1024)S(1)} %pad_clamp_fusion.1), kind=kCustom, calls=%fused_computation.clone | custom fusion | bytes 9437760 | tf_op jit(solution)/shard_map/jit(_take)/gather | solution.py:15
  53.8 9.9 %gather_fusion.2 = bf16[144,128,128]{2,1,0:T(8,128)(2,1)} fusion(bf16[128,144,128]{2,0,1:T(8,128)(2,1)} %copy.20, s32[1024]{0:T(1024)S(1)} %pad_clamp_fusion.1), kind=kCustom, calls=%fused_computation.1.clone | custom fusion | bytes 9437760 | tf_op jit(solution)/shard_map/jit(_take)/gather | solution.py:15
  63.7 8.7 %select_bitcast_fusion.1 = (bf16[128,144,128]{2,0,1:T(8,128)(2,1)}, bf16[128,144,128]{2,0,1:T(8,128)(2,1)}) fusion(bf16[144,128,128]{2,1,0:T(8,128)(2,1)} %gather_fusion.1, pred[144]{0:T(512)(128)(4,1)S(1)} %compare_and_fusion, bf16[144,128,128]{2,1,0:T(8,128)(2,1)} %gather_fusion.2), kind=kLoop, calls=%fused_computation.16 | loop fusion | flops 4718592 | bytes 18874512 | tf_op jit(solution)/shard_map/jit(_take)/select_n | solution.py:15
  72.3 6.7 %copy.15 = bf16[128,144,128]{0,2,1:T(8,128)(2,1)} copy(bf16[128,144,128]{2,0,1:T(8,128)(2,1)} %get-tuple-element.12) | data formatting | bytes 9437184 | tf_op jit(solution)/shard_map/jit(_take)/select_n | solution.py:15
  79.0 7.3 %all-to-all-start = ((bf16[128,16,1152]{0,2,1:T(8,128)(2,1)}), bf16[128,16,1152]{0,2,1:T(8,128)(2,1)}, u32[]{:S(2)}, u32[]{:S(2)}) async-start(bf16[128,16,1152]{0,2,1:T(8,128)(2,1)} %bitcast.64), calls=%async_computation | async-start | bytes 9437184 | tf_op jit(solution)/shard_map/all_to_all | solution.py:38
  86.3 6.6 %copy.21 = bf16[128,144,128]{0,2,1:T(8,128)(2,1)} copy(bf16[128,144,128]{2,0,1:T(8,128)(2,1)} %get-tuple-element.13) | data formatting | bytes 9437184 | tf_op jit(solution)/shard_map/jit(_take)/select_n | solution.py:15
  92.9 63.9 %all-to-all-done = bf16[128,16,1152]{0,2,1:T(8,128)(2,1)} async-done(((bf16[128,16,1152]{0,2,1:T(8,128)(2,1)}), bf16[128,16,1152]{0,2,1:T(8,128)(2,1)}, u32[]{:S(2)}, u32[]{:S(2)}) %all-to-all-start) | async-done | bytes 4718624 | tf_op jit(solution)/shard_map/all_to_all | solution.py:38
  156.9 5.0 %all-to-all-start.1 = ((bf16[128,16,1152]{0,2,1:T(8,128)(2,1)}), bf16[128,16,1152]{0,2,1:T(8,128)(2,1)}, u32[]{:S(2)}, u32[]{:S(2)}) async-start(bf16[128,16,1152]{0,2,1:T(8,128)(2,1)} %bitcast.63), calls=%async_computation.1 | async-start | bytes 9437184 | tf_op jit(solution)/shard_map/all_to_all | solution.py:38
  161.9 0.0 copy-done.1
  161.9 0.1 compare_and_fusion.1
  162.0 0.0 copy-done
  162.0 83.7 %all_gather.7 = bf16[2,64,2048]{2,1,0:T(8,128)(2,1)S(1)} all-gather(bf16[2,64,128]{2,1,0:T(8,128)(2,1)S(1)} %copy-done), channel_id=1, replica_groups=mesh['fsdp'=8,'tp'=16] {'tp'}, dimensions={2}, use_global_device_ids=true | all-gather | bytes 557056 | tf_op jit(solution)/shard_map/all_gather | solution.py:32
  245.7 0.0 all-gather.2.cloned.1.call-done
  245.8 5.9 %copy_bitcast_fusion = bf16[2,64,144,128]{3,1,2,0:T(8,128)(2,1)} fusion(bf16[2,64,18432]{2,1,0:T(8,128)(2,1)} %all-gather.2.cloned.1.call-done), kind=kLoop, calls=%fused_computation.14 | loop fusion | bytes 9437184 | tf_op jit(solution)/shard_map/reshape | solution.py:14
  251.7 2.9 gather_fusion
  254.6 0.1 select_bitcast_fusion.2
  254.7 0.1 copy.18
  254.9 0.1 copy.23
  255.0 6.0 %fusion.2 = bf16[1,2048,1152]{1,2,0:T(8,128)(2,1)} fusion(bf16[2,64,2048]{2,1,0:T(8,128)(2,1)S(1)} %all_gather.7, bf16[8,8,9,128]{3,2,1,0:T(8,128)(2,1)S(1)} %bitcast.68, bf16[128,16,1152]{0,2,1:T(8,128)(2,1)} %all-to-all-done), kind=kOutput, calls=%fused_computation.12 | convolution fusion | flops 311427072 | bytes 9961472 | tf_op jit(solution)/shard_map/dot_general | solution.py:20
  260.9 0.0 all-to-all-done.1
  260.9 5.9 %fusion.3 = bf16[1,2048,1152]{1,2,0:T(8,128)(2,1)} fusion(bf16[2,64,2048]{2,1,0:T(8,128)(2,1)S(1)} %all_gather.7, bf16[8,8,9,128]{3,2,1,0:T(8,128)(2,1)S(1)} %bitcast.67, bf16[128,16,1152]{0,2,1:T(8,128)(2,1)} %all-to-all-done.1), kind=kOutput, calls=%fused_computation.13 | convolution fusion | flops 311427072 | bytes 9961472 | tf_op jit(solution)/shard_map/dot_general | solution.py:20
  266.9 8.3 %pad_maximum_fusion = bf16[2,2048,1152]{1,2,0:T(8,128)(2,1)} fusion(bf16[1,2048,1152]{1,2,0:T(8,128)(2,1)} %fusion.3, bf16[1,2048,1152]{1,2,0:T(8,128)(2,1)} %fusion.2), kind=kLoop, calls=%fused_computation.9 | loop fusion | flops 4718592 | bytes 18874368 | tf_op jit(solution)/shard_map/stack | solution.py:42
  275.2 12.6 %copy.24 = bf16[2,2048,1152]{2,1,0:T(8,128)(2,1)} copy(bf16[2,2048,1152]{1,2,0:T(8,128)(2,1)} %pad_maximum_fusion) | data formatting | bytes 18874368 | tf_op jit(solution)/shard_map/stack | solution.py:42
  (5 shorter events, 0.0 us)
Async XLA Ops:
  6.5 239.2 %all-gather.2.cloned.1.call-start = ((), (), s32[]{:S(2)}) async-start(), calls=%async_computation.2 | async-start | bytes 5308416 | tf_op jit(solution)/shard_map/all_gather | solution.py:34
  79.0 77.9 %all-to-all-start = ((bf16[128,16,1152]{0,2,1:T(8,128)(2,1)}), bf16[128,16,1152]{0,2,1:T(8,128)(2,1)}, u32[]{:S(2)}, u32[]{:S(2)}) async-start(bf16[128,16,1152]{0,2,1:T(8,128)(2,1)} %bitcast.64), calls=%async_computation | async-start | bytes 9437184 | tf_op jit(solution)/shard_map/all_to_all | solution.py:38
  156.9 5.0 %copy-start.1 = (s32[144]{0:T(256)S(1)}, s32[144]{0:T(256)}, u32[]{:S(2)}) copy-start(s32[144]{0:T(256)} %param.9) | copy-start | bytes 1732
  156.9 5.1 %copy-start = (bf16[2,64,128]{2,1,0:T(8,128)(2,1)S(1)}, bf16[2,64,128]{2,1,0:T(8,128)(2,1)}, u32[]{:S(2)}) copy-start(bf16[2,64,128]{2,1,0:T(8,128)(2,1)} %param.7) | copy-start | bytes 98308
  156.9 104.0 %all-to-all-start.1 = ((bf16[128,16,1152]{0,2,1:T(8,128)(2,1)}), bf16[128,16,1152]{0,2,1:T(8,128)(2,1)}, u32[]{:S(2)}, u32[]{:S(2)}) async-start(bf16[128,16,1152]{0,2,1:T(8,128)(2,1)} %bitcast.63), calls=%async_computation.1 | async-start | bytes 9437184 | tf_op jit(solution)/shard_map/all_to_all | solution.py:38
Sparse Core Ops, SparseCore 0:
  9.0 36.9 all-gather.1
where the time goes:
time: 297 us; the launch traced here: 295 us
  local copies, waits for them, and re-layouts  90 us (30%)
  blocking collectives  83.7 us (28%)
  waiting for transfers between devices  64.7 us (22%)
  other arithmetic  18.5 us (6%)
  between operations  13.5 us (5%)
  starting transfers between devices  12.3 us (4%)
  matrix products  11.9 us (4%)
    all_gather x1, blocking collectives, per_device(): lax.all_gather(down_factor_transposed, 'tp', axis=2, tiled=True)  83.7 us
    all_to_all x2, waiting for transfers between devices, per_device(): lax.all_to_all(ordered, 'tp', split_axis=1, concat_axis=0, tiled=True)  63.9 us
    gather x3, local copies, waits for them, and re-layouts, permute_columns(): blocks = jnp.take(blocks, order, axis=-2)  22.8 us
    another operation x2, local copies, waits for them, and re-layouts, permute_columns(): blocks = values.reshape(lead + (values.shape[-1] // BLOCK, BLOCK))  13.4 us
    select_n x2, local copies, waits for them, and re-layouts, permute_columns(): blocks = jnp.take(blocks, order, axis=-2)  13.3 us
    unnamed x6, local copies, waits for them, and re-layouts  13.3 us
    another operation x1, local copies, waits for them, and re-layouts, per_device(): return jnp.stack(merged_outputs)  12.6 us
    all_to_all x2, starting transfers between devices, per_device(): lax.all_to_all(ordered, 'tp', split_axis=1, concat_axis=0, tiled=True)  12.3 us
  transfers between devices with their start and end apart: 3, of which 1 were waited for; matrix products, arithmetic and copies ran while one was open for 32% of the time, Pallas kernels for 0%

commit v1 on v0

v1 whole, which is shorter than its diff:
```python
import jax
import jax.numpy as jnp
from jax import lax
from jax.experimental import pallas as pl
from jax.experimental.pallas import tpu as pltpu
from jax.sharding import PartitionSpec as P

BLOCK = 128
STRIPE = 32
VMEM_BYTES = 60 << 20


def block_at(order, j):
    return pl.ds(pl.multiple_of(order[j] * BLOCK, BLOCK), BLOCK)


def pack(order, base, down, servers):
    layers, rows, columns = base.shape
    per_server = order.shape[0] // servers
    chunk = layers * per_server + 1
    stripes = rows // STRIPE

    def kernel(order, base, down, out, held, packed, load_sem, store_sem):
        def load(s):
            return pltpu.make_async_copy(
                base.at[s // stripes, pl.ds(s % stripes * STRIPE, STRIPE)], held.at[s], load_sem.at[s]
            )

        def store(blocks, at):
            return pltpu.make_async_copy(packed.at[:, blocks, at], out.at[:, blocks, at], store_sem.at[0])

        for s in range(layers * stripes):
            load(s).start()
        for d in range(servers):
            packed[d, chunk - 1] = down[...]
        store(pl.ds(chunk - 1, 1), pl.ds(0, rows)).start()
        for s in range(layers * stripes):
            layer, at = s // stripes, pl.ds(s % stripes * STRIPE, STRIPE)
            load(s).wait()

            @pl.loop(0, servers)
            def _(d):
                for c in range(per_server):
                    packed[d, layer * per_server + c, at] = held[s, :, block_at(order, d * per_server + c)]

            store(pl.ds(layer * per_server, per_server), at).start()
        pltpu.make_async_copy(packed, out, store_sem.at[0]).wait()

    return pl.pallas_call(
        kernel,
        out_shape=jax.ShapeDtypeStruct((servers, chunk, rows, BLOCK), jnp.bfloat16),
        in_specs=[
            pl.BlockSpec(memory_space=pltpu.SMEM),
            pl.BlockSpec(memory_space=pltpu.HBM),
            pl.BlockSpec(memory_space=pltpu.VMEM),
        ],
        out_specs=pl.BlockSpec(memory_space=pltpu.HBM),
        scratch_shapes=[
            pltpu.VMEM((layers * stripes, STRIPE, columns), jnp.bfloat16),
            pltpu.VMEM((servers, chunk, rows, BLOCK), jnp.bfloat16),
            pltpu.SemaphoreType.DMA((layers * stripes,)),
            pltpu.SemaphoreType.DMA((1,)),
        ],
        compiler_params=pltpu.CompilerParams(vmem_limit_bytes=VMEM_BYTES),
        name="pack",
    )(order, base, down)


def merge(order, received, up):
    servers, chunk, rows, _ = received.shape
    layers, ranks, _ = up.shape
    per_server = (chunk - 1) // layers
    width = per_server * BLOCK

    def kernel(order, received, up, out, chosen, held, merged, up_sem, load_sem, store_sem):
        first = lax.axis_index("tp") * per_server
        for c in range(per_server):
            pltpu.make_async_copy(
                up.at[:, :, block_at(order, first + c)],
                chosen.at[:, :, pl.ds(c * BLOCK, BLOCK)],
                up_sem.at[0],
            ).start()

        def load(s):
            return pltpu.make_async_copy(received.at[s], held.at[s], load_sem.at[s])

        for s in range(servers):
            load(s).start()
        pltpu.make_async_copy(chosen, chosen, up_sem.at[0]).wait()

        @pl.loop(0, servers)
        def _(s):
            load(s).wait()
            at = pl.ds(pl.multiple_of(s * rows, rows), rows)
            for layer in range(layers):
                delta = lax.dot_general(
                    held[s, chunk - 1, layer * ranks : (layer + 1) * ranks] * jnp.bfloat16(2),
                    chosen[layer],
                    (((0,), (0,)), ((), ())),
                    preferred_element_type=jnp.float32,
                )
                for c in range(per_server):
                    columns = slice(c * BLOCK, (c + 1) * BLOCK)
                    base = held[s, layer * per_server + c].astype(jnp.float32)
                    merged[layer, at, columns] = (base + delta[:, columns]).astype(jnp.bfloat16)
            pltpu.make_async_copy(merged.at[:, at], out.at[:, at], store_sem.at[0]).start()

        pltpu.make_async_copy(merged, out, store_sem.at[0]).wait()

    return pl.pallas_call(
        kernel,
        out_shape=jax.ShapeDtypeStruct((layers, servers * rows, width), jnp.bfloat16),
        in_specs=[
            pl.BlockSpec(memory_space=pltpu.SMEM),
            pl.BlockSpec(memory_space=pltpu.HBM),
            pl.BlockSpec(memory_space=pltpu.HBM),
        ],
        out_specs=pl.BlockSpec(memory_space=pltpu.HBM),
        scratch_shapes=[
            pltpu.VMEM((layers, ranks, width), jnp.bfloat16),
            pltpu.VMEM((servers, chunk, rows, BLOCK), jnp.bfloat16),
            pltpu.VMEM((layers, servers * rows, width), jnp.bfloat16),
            pltpu.SemaphoreType.DMA((1,)),
            pltpu.SemaphoreType.DMA((servers,)),
            pltpu.SemaphoreType.DMA((1,)),
        ],
        compiler_params=pltpu.CompilerParams(vmem_limit_bytes=VMEM_BYTES),
        name="merge",
    )(order, received, up)


def per_device(base_projection, down_factor_transposed, up_factor, block_permutation):
    servers = lax.axis_size("tp")
    up = lax.all_gather(up_factor, "fsdp", axis=1, tiled=True)
    packed = pack(block_permutation, base_projection, down_factor_transposed.reshape(-1, BLOCK), servers)
    received = lax.cond(
        lax.axis_index("tp") < servers,
        lambda sent: lax.all_to_all(sent, "tp", split_axis=0, concat_axis=0, tiled=True),
        lambda sent: jnp.zeros_like(sent),
        packed,
    )
    return merge(block_permutation, received, up)


def solution(mesh):
    return jax.shard_map(
        per_device,
        mesh=mesh,
        in_specs=(
            P(None, ("fsdp", "tp"), None),
            P(None, None, ("fsdp", "tp")),
            P(None, "fsdp", None),
            P(),
        ),
        out_specs=P(None, "fsdp", "tp"),
        check_vma=False,
    )
```

time: 297 us -> 154 us (0.52)
  local copies, waits for them, and re-layouts: 90 us -> 0 us
  waiting for transfers between devices: 64.7 us -> 0.71 us
  blocking collectives: 83.7 us -> 120 us
  Pallas kernels: 0 us -> 19.6 us
  other arithmetic: 18.5 us -> 0 us
  starting transfers between devices: 12.3 us -> 0.01 us
  matrix products: 11.9 us -> 0 us
    all_to_all x0 -> x1, blocking collectives: none -> 120 us  [per_device(): lax.all_to_all(sent, 'tp', split_axis=0, concat_axis=0, tiled=True)]
    all_gather x1 -> x0, blocking collectives: 83.7 us -> none  [per_device(): lax.all_gather(down_factor_transposed, 'tp', axis=2, tiled=True)]
    all_to_all x2 -> x0, waiting for transfers between devices: 63.9 us -> none  [per_device(): lax.all_to_all(ordered, 'tp', split_axis=1, concat_axis=0, tiled=True)]
    another operation x3 -> x0, local copies, waits for them, and re-layouts: 26 us -> none  [the longest x2 13.4 us: permute_columns(): blocks = values.reshape(lead + (values.shape[-1] // BLOCK, BLOCK))]
    gather x3 -> x0, local copies, waits for them, and re-layouts: 22.8 us -> none  [permute_columns(): blocks = jnp.take(blocks, order, axis=-2)]
    pallas_call x0 -> x2, Pallas kernels: none -> 19.6 us  [the longest x1 10.9 us: merge(): pl.pallas_call(kernel, out_shape=jax.ShapeDtypeStruct((layers, servers *...]
    select_n x2 -> x0, local copies, waits for them, and re-layouts: 13.3 us -> none  [permute_columns(): blocks = jnp.take(blocks, order, axis=-2)]
    unnamed x6 -> x0, local copies, waits for them, and re-layouts: 13.3 us -> none
  transfers between devices with their start and end apart: 3 -> 1, of which waited for: 1 -> 0; matrix products, arithmetic and copies ran while one was open for 32% -> 0% of each run, Pallas kernels for 0% -> 6%
where the time goes in v1:
time: 154 us
  blocking collectives  120 us (78%)
  Pallas kernels  19.6 us (13%)
  between operations  13.4 us (9%)
    all_to_all x1, blocking collectives, per_device(): lax.all_to_all(sent, 'tp', split_axis=0, concat_axis=0, tiled=True)  120 us
    pallas_call x1, Pallas kernels, merge(): pl.pallas_call(kernel, out_shape=jax.ShapeDtypeStruct((layers, servers *...  10.9 us
    pallas_call x1, Pallas kernels, pack(): pl.pallas_call(kernel, out_shape=jax.ShapeDtypeStruct((servers, chunk, ro...  8.72 us
  transfers between devices with their start and end apart: 1, of which 0 were waited for; matrix products, arithmetic and copies ran while one was open for 0% of the time, Pallas kernels for 6%

profile of v1, /device:TPU:0, one launch (start us, length us, event | category | flops | bytes accessed | tf_op | source)
XLA Modules:
  0.0 153.6 jit_solution(8695976467508701079)
XLA Ops:
  6.5 0.0 all-gather.2.cloned.1.call-start
  6.5 0.7 all-gather.2.cloned.1.call-update
  7.3 8.7 %pack.1 = bf16[16,19,128,128]{3,2,1,0:T(8,128)(2,1)} custom-call(s32[144]{0:T(256)} %order.3, bf16[2,128,18432]{2,1,0:T(8,128)(2,1)} %base.1, bf16[128,128]{1,0:T(8,128)(2,1)} %bitcast.1), custom_call_target="tpu_custom_call" | custom-call | tf_op jit(solution)/shard_map/pack/pallas_call | solution.py:49
  16.0 119.9 %conditional.1 = (bf16[16,19,128,128]{3,2,1,0:T(8,128)(2,1)}) conditional(s32[]{:T(128)} %convert_element_type.3, () %tuple.11, bf16[16,19,128,128]{3,2,1,0:T(8,128)(2,1)} %pack.1), branch_computations={%region_0.0_spmd, %region_1.0_spmd} | conditional | bytes 19922952 | solution.py:136
  16.0 119.9 %all_to_all.4 = bf16[16,19,128,128]{3,2,1,0:T(8,128)(2,1)} all-to-all(bf16[16,19,128,128]{3,2,1,0:T(8,128)(2,1)} %param.1), channel_id=1, replica_groups=mesh['fsdp'=8,'tp'=16] {'tp'}, dimensions={0} | all-to-all | bytes 19922944 | tf_op jit(solution)/shard_map/cond/branch_1_fun/all_to_all | solution.py:138
  135.9 0.0 all-gather.2.cloned.1.call-done.up
  135.9 10.9 %merge.1 = bf16[2,2048,1152]{2,1,0:T(8,128)(2,1)} custom-call(s32[144]{0:T(256)} %order.3, bf16[16,19,128,128]{3,2,1,0:T(8,128)(2,1)} %get-tuple-element.9.received, bf16[2,64,18432]{2,1,0:T(8,128)(2,1)} %all-gather.2.cloned.1.call-done.up), custom_call_target="tpu_custom_call" | custom-call | tf_op jit(solution)/shard_map/merge/pallas_call | solution.py:110
Async XLA Ops:
  6.5 129.3 %all-gather.2.cloned.1.call-start = ((), (), s32[]{:S(2)}) async-start(), calls=%async_computation.1 | async-start | bytes 5308416 | tf_op jit(solution)/shard_map/all_gather | solution.py:134
Sparse Core Ops, SparseCore 0:
  9.0 36.9 all-gather.1

commit v2 on v1

v2 whole, which is shorter than its diff:
```python
import jax
import jax.numpy as jnp
from jax import lax
from jax.experimental import pallas as pl
from jax.experimental.pallas import tpu as pltpu
from jax.sharding import PartitionSpec as P

BLOCK = 128
STRIPE = 32
SOURCES = 2
COLUMNS = 3


def block_at(order, j):
    return pl.ds(pl.multiple_of(order[j] * BLOCK, BLOCK), BLOCK)


def pack(order, base, down, servers):
    layers, rows, columns = base.shape
    per_server = order.shape[0] // servers
    chunk = layers * per_server + 1
    stripes = rows // STRIPE

    def kernel(order, base, down, packed, held, load_sem):
        def load(s):
            return pltpu.make_async_copy(
                base.at[s // stripes, pl.ds(s % stripes * STRIPE, STRIPE)], held.at[s], load_sem.at[s]
            )

        for s in range(layers * stripes):
            load(s).start()
        for d in range(servers):
            packed[d, chunk - 1] = down[...]
        for s in range(layers * stripes):
            layer, at = s // stripes, pl.ds(s % stripes * STRIPE, STRIPE)
            load(s).wait()

            @pl.loop(0, servers)
            def _(d):
                for c in range(per_server):
                    packed[d, layer * per_server + c, at] = held[s, :, block_at(order, d * per_server + c)]

    return pl.pallas_call(
        kernel,
        out_shape=pltpu.VMEM((servers, chunk, rows, BLOCK), jnp.bfloat16),
        in_specs=[
            pl.BlockSpec(memory_space=pltpu.SMEM),
            pl.BlockSpec(memory_space=pltpu.HBM),
            pl.BlockSpec(memory_space=pltpu.VMEM),
        ],
        out_specs=pl.BlockSpec(memory_space=pltpu.VMEM),
        scratch_shapes=[
            pltpu.VMEM((layers * stripes, STRIPE, columns), jnp.bfloat16),
            pltpu.SemaphoreType.DMA((layers * stripes,)),
        ],
        compiler_params=pltpu.CompilerParams(vmem_limit_bytes=40 << 20),
        name="pack",
    )(order, base, down)


def merge(order, received, up):
    servers, chunk, rows, _ = received.shape
    layers, ranks, _ = up.shape
    per_server = (chunk - 1) // layers
    width = per_server * BLOCK

    def kernel(order, received, up, out, chosen, held, merged, up_sem, load_sem, store_sem):
        first = lax.axis_index("tp") * per_server
        for c in range(per_server):
            pltpu.make_async_copy(
                up.at[:, :, block_at(order, first + c)],
                chosen.at[:, :, pl.ds(c * BLOCK, BLOCK)],
                up_sem.at[0],
            ).start()

        def load(s):
            return pltpu.make_async_copy(received.at[s], held.at[s], load_sem.at[s])

        for s in range(servers):
            load(s).start()
        pltpu.make_async_copy(chosen, chosen, up_sem.at[0]).wait()

        @pl.loop(0, servers // SOURCES)
        def _(step):
            sources = [step * SOURCES + i for i in range(SOURCES)]
            for s in sources:
                load(s).wait()
            for layer in range(layers):
                down = jnp.concatenate(
                    [held[s, chunk - 1, layer * ranks : (layer + 1) * ranks] for s in sources], axis=1
                ) * jnp.bfloat16(2)
                for c in range(0, per_server, COLUMNS):
                    delta = lax.dot_general(
                        down,
                        chosen[layer, :, c * BLOCK : (c + COLUMNS) * BLOCK],
                        (((0,), (0,)), ((), ())),
                        preferred_element_type=jnp.float32,
                    )
                    for i, s in enumerate(sources):
                        for j in range(COLUMNS):
                            base = held[s, layer * per_server + c + j].astype(jnp.float32)
                            part = delta[i * rows : (i + 1) * rows, j * BLOCK : (j + 1) * BLOCK]
                            at = pl.ds(pl.multiple_of(s * rows, rows), rows)
                            merged[layer, at, (c + j) * BLOCK : (c + j + 1) * BLOCK] = (base + part).astype(jnp.bfloat16)
            at = pl.ds(pl.multiple_of(step * SOURCES * rows, rows), SOURCES * rows)
            pltpu.make_async_copy(merged.at[:, at], out.at[:, at], store_sem.at[0]).start()

        pltpu.make_async_copy(merged, out, store_sem.at[0]).wait()

    return pl.pallas_call(
        kernel,
        out_shape=jax.ShapeDtypeStruct((layers, servers * rows, width), jnp.bfloat16),
        in_specs=[
            pl.BlockSpec(memory_space=pltpu.SMEM),
            pl.BlockSpec(memory_space=pltpu.HBM),
            pl.BlockSpec(memory_space=pltpu.HBM),
        ],
        out_specs=pl.BlockSpec(memory_space=pltpu.HBM),
        scratch_shapes=[
            pltpu.VMEM((layers, ranks, width), jnp.bfloat16),
            pltpu.VMEM((servers, chunk, rows, BLOCK), jnp.bfloat16),
            pltpu.VMEM((layers, servers * rows, width), jnp.bfloat16),
            pltpu.SemaphoreType.DMA((1,)),
            pltpu.SemaphoreType.DMA((servers,)),
            pltpu.SemaphoreType.DMA((1,)),
        ],
        compiler_params=pltpu.CompilerParams(vmem_limit_bytes=60 << 20),
        name="merge",
    )(order, received, up)


def per_device(base_projection, down_factor_transposed, up_factor, block_permutation):
    servers = lax.axis_size("tp")
    up = lax.all_gather(up_factor, "fsdp", axis=1, tiled=True)
    down = down_factor_transposed.reshape(-1, BLOCK)

    def exchange(order, base, down):
        packed = pack(order, base, down, servers)
        return lax.all_to_all(packed, "tp", split_axis=0, concat_axis=0, tiled=True)

    def nothing(order, base, down):
        layers, rows, columns = base.shape
        blocks = layers * columns // BLOCK // servers + 1
        return jnp.zeros((servers, blocks, rows, BLOCK), jnp.bfloat16)

    received = lax.cond(
        lax.axis_index("tp") < servers, exchange, nothing, block_permutation, base_projection, down
    )
    return merge(block_permutation, received, up)


def solution(mesh):
    return jax.shard_map(
        per_device,
        mesh=mesh,
        in_specs=(
            P(None, ("fsdp", "tp"), None),
            P(None, None, ("fsdp", "tp")),
            P(None, "fsdp", None),
            P(),
        ),
        out_specs=P(None, "fsdp", "tp"),
        check_vma=False,
    )
```

time: 154 us -> 149 us (0.968)
  Pallas kernels: 19.6 us -> 14.9 us
    pallas_call x1, Pallas kernels: 8.72 us -> 5.41 us  [pack(): pl.pallas_call(kernel, out_shape=pltpu.VMEM((servers, chunk, rows, BLOCK)...]
  transfers between devices with their start and end apart: 1 -> 1, of which waited for: 0 -> 0; matrix products, arithmetic and copies ran while one was open for 0% -> 0% of each run, Pallas kernels for 6% -> 4%
where the time goes in v2:
time: 149 us
  blocking collectives  120 us (81%)
  Pallas kernels  14.9 us (10%)
  between operations  13.4 us (9%)
    all_to_all x1, blocking collectives, exchange(): return lax.all_to_all(packed, 'tp', split_axis=0, concat_axis=0, tiled=True)  120 us
    pallas_call x1, Pallas kernels, merge(): pl.pallas_call(kernel, out_shape=jax.ShapeDtypeStruct((layers, servers *...  9.52 us
    pallas_call x1, Pallas kernels, pack(): pl.pallas_call(kernel, out_shape=pltpu.VMEM((servers, chunk, rows, BLOCK)...  5.41 us
  transfers between devices with their start and end apart: 1, of which 0 were waited for; matrix products, arithmetic and copies ran while one was open for 0% of the time, Pallas kernels for 4%

profile of v2, /device:TPU:0, one launch (start us, length us, event | category | flops | bytes accessed | tf_op | source)
XLA Modules:
  0.0 148.8 jit_solution(10439912073784807495)
XLA Ops:
  6.5 0.0 all-gather.2.cloned.1.call-start
  6.5 0.7 all-gather.2.cloned.1.call-update
  7.3 125.1 %conditional.1 = (bf16[16,19,128,128]{3,2,1,0:T(8,128)(2,1)}) conditional(s32[]{:T(128)} %convert_element_type.3, () %tuple.11, (s32[144]{0:T(256)}, bf16[2,128,18432]{2,1,0:T(8,128)(2,1)}, bf16[2,64,128]{2,1,0:T(8,128)(2,1)}) %tuple.12), branch_computations={%region_0.0_spmd, %region_1.0_spmd} | conditional | bytes 19922952 | solution.py:146
  7.3 5.4 %pack.1 = bf16[16,19,128,128]{3,2,1,0:T(8,128)(2,1)S(1)} custom-call(s32[144]{0:T(256)} %get-tuple-element.14.order, bf16[2,128,18432]{2,1,0:T(8,128)(2,1)} %get-tuple-element.19.base, bf16[128,128]{1,0:T(8,128)(2,1)} %bitcast.1), custom_call_target="tpu_custom_call" | custom-call | tf_op jit(solution)/shard_map/cond/branch_1_fun/pack/pallas_call | solution.py:43
  12.7 119.7 %all_to_all.4 = bf16[16,19,128,128]{3,2,1,0:T(8,128)(2,1)} all-to-all(bf16[16,19,128,128]{3,2,1,0:T(8,128)(2,1)S(1)} %pack.1), channel_id=1, replica_groups=mesh['fsdp'=8,'tp'=16] {'tp'}, dimensions={0} | all-to-all | bytes 19922944 | tf_op jit(solution)/shard_map/cond/branch_1_fun/all_to_all | solution.py:139
  132.4 0.0 all-gather.2.cloned.1.call-done.up
  132.4 9.5 %merge.1 = bf16[2,2048,1152]{2,1,0:T(8,128)(2,1)} custom-call(s32[144]{0:T(256)} %order.1, bf16[16,19,128,128]{3,2,1,0:T(8,128)(2,1)} %get-tuple-element.22.received, bf16[2,64,18432]{2,1,0:T(8,128)(2,1)} %all-gather.2.cloned.1.call-done.up), custom_call_target="tpu_custom_call" | custom-call | tf_op jit(solution)/shard_map/merge/pallas_call | solution.py:110
Async XLA Ops:
  6.5 125.8 %all-gather.2.cloned.1.call-start = ((), (), s32[]{:S(2)}) async-start(), calls=%async_computation.1 | async-start | bytes 5308416 | tf_op jit(solution)/shard_map/all_gather | solution.py:134
Sparse Core Ops, SparseCore 0:
  9.0 36.9 all-gather.1

commit v3 on v2

v3 whole, which is shorter than its diff:
```python
import jax
import jax.numpy as jnp
from jax import lax
from jax.experimental import pallas as pl
from jax.experimental.pallas import tpu as pltpu
from jax.sharding import PartitionSpec as P

BLOCK = 128
STRIPE = 32
SOURCES = 4
COLUMNS = 3


def block_at(order, j):
    return pl.ds(pl.multiple_of(order[j] * BLOCK, BLOCK), BLOCK)


def pack(order, base, servers):
    layers, rows, columns = base.shape
    per_server = order.shape[0] // servers
    chunk = layers * per_server
    stripes = rows // STRIPE

    def kernel(order, base, packed, held, load_sem):
        def load(s):
            return pltpu.make_async_copy(
                base.at[s // stripes, pl.ds(s % stripes * STRIPE, STRIPE)], held.at[s], load_sem.at[s]
            )

        for s in range(layers * stripes):
            load(s).start()
        for s in range(layers * stripes):
            layer, at = s // stripes, pl.ds(s % stripes * STRIPE, STRIPE)
            load(s).wait()

            @pl.loop(0, servers, unroll=4)
            def _(d):
                for c in range(per_server):
                    packed[d, layer * per_server + c, at] = held[s, :, block_at(order, d * per_server + c)]

    return pl.pallas_call(
        kernel,
        out_shape=pltpu.VMEM((servers, chunk, rows, BLOCK), jnp.bfloat16),
        in_specs=[
            pl.BlockSpec(memory_space=pltpu.SMEM),
            pl.BlockSpec(memory_space=pltpu.HBM),
        ],
        out_specs=pl.BlockSpec(memory_space=pltpu.VMEM),
        scratch_shapes=[
            pltpu.VMEM((layers * stripes, STRIPE, columns), jnp.bfloat16),
            pltpu.SemaphoreType.DMA((layers * stripes,)),
        ],
        compiler_params=pltpu.CompilerParams(vmem_limit_bytes=40 << 20),
        name="pack",
    )(order, base)


def merge(order, received, up, down):
    servers, chunk, rows, _ = received.shape
    layers, ranks, _ = up.shape
    per_server = chunk // layers
    width = per_server * BLOCK

    def kernel(order, received, up, downs, out, chosen, factor, held, merged, up_sem, down_sem, load_sem, store_sem):
        first = lax.axis_index("tp") * per_server
        for c in range(per_server):
            pltpu.make_async_copy(
                up.at[:, :, block_at(order, first + c)],
                chosen.at[:, :, pl.ds(c * BLOCK, BLOCK)],
                up_sem.at[0],
            ).start()

        rank_rows = pl.ds(lax.axis_index("fsdp") % 2 * servers, servers)
        load_down = pltpu.make_async_copy(downs.at[rank_rows], factor, down_sem.at[0])
        load_down.start()

        def load(s):
            return pltpu.make_async_copy(received.at[s], held.at[s], load_sem.at[s])

        for s in range(servers):
            load(s).start()
        pltpu.make_async_copy(chosen, chosen, up_sem.at[0]).wait()
        load_down.wait()

        @pl.loop(0, servers // SOURCES)
        def _(step):
            sources = [step * SOURCES + i for i in range(SOURCES)]
            for s in sources:
                load(s).wait()
            for layer in range(layers):
                down = jnp.concatenate(
                    [factor[s, layer * ranks : (layer + 1) * ranks] for s in sources], axis=1
                ) * jnp.bfloat16(2)
                for c in range(0, per_server, COLUMNS):
                    delta = lax.dot_general(
                        down,
                        chosen[layer, :, c * BLOCK : (c + COLUMNS) * BLOCK],
                        (((0,), (0,)), ((), ())),
                        preferred_element_type=jnp.float32,
                    )
                    for i, s in enumerate(sources):
                        for j in range(COLUMNS):
                            base = held[s, layer * per_server + c + j].astype(jnp.float32)
                            part = delta[i * rows : (i + 1) * rows, j * BLOCK : (j + 1) * BLOCK]
                            at = pl.ds(pl.multiple_of(s * rows, rows), rows)
                            merged[layer, at, (c + j) * BLOCK : (c + j + 1) * BLOCK] = (base + part).astype(jnp.bfloat16)
                at = pl.ds(pl.multiple_of(step * SOURCES * rows, rows), SOURCES * rows)
                pltpu.make_async_copy(merged.at[layer, at], out.at[layer, at], store_sem.at[0]).start()

        pltpu.make_async_copy(merged, out, store_sem.at[0]).wait()

    return pl.pallas_call(
        kernel,
        out_shape=jax.ShapeDtypeStruct((layers, servers * rows, width), jnp.bfloat16),
        in_specs=[
            pl.BlockSpec(memory_space=pltpu.SMEM),
            pl.BlockSpec(memory_space=pltpu.HBM),
            pl.BlockSpec(memory_space=pltpu.HBM),
            pl.BlockSpec(memory_space=pltpu.HBM),
        ],
        out_specs=pl.BlockSpec(memory_space=pltpu.HBM),
        scratch_shapes=[
            pltpu.VMEM((layers, ranks, width), jnp.bfloat16),
            pltpu.VMEM((servers, layers * ranks, rows), jnp.bfloat16),
            pltpu.VMEM((servers, chunk, rows, BLOCK), jnp.bfloat16),
            pltpu.VMEM((layers, servers * rows, width), jnp.bfloat16),
            pltpu.SemaphoreType.DMA((1,)),
            pltpu.SemaphoreType.DMA((1,)),
            pltpu.SemaphoreType.DMA((servers,)),
            pltpu.SemaphoreType.DMA((1,)),
        ],
        compiler_params=pltpu.CompilerParams(vmem_limit_bytes=60 << 20),
        name="merge",
    )(order, received, up, down)


def per_device(base_projection, down_factor_transposed, up_factor, block_permutation):
    servers = lax.axis_size("tp")
    up = lax.all_gather(up_factor, "fsdp", axis=1, tiled=True)
    layers, ranks, rows = down_factor_transposed.shape
    pairs = lax.axis_size("fsdp") // 2
    group = 2 * servers
    down = lax.all_gather(
        down_factor_transposed.reshape(layers * ranks, rows),
        ("fsdp", "tp"),
        axis=0,
        tiled=True,
        axis_index_groups=[[p * group + i for i in range(group)] for p in range(pairs)],
    ).reshape(group, layers * ranks, rows)

    def exchange(order, base):
        packed = pack(order, base, servers)
        return lax.all_to_all(packed, "tp", split_axis=0, concat_axis=0, tiled=True)

    def nothing(order, base):
        blocks = layers * base.shape[2] // BLOCK // servers
        return jnp.zeros((servers, blocks, rows, BLOCK), jnp.bfloat16)

    received = lax.cond(lax.axis_index("tp") < servers, exchange, nothing, block_permutation, base_projection)
    return merge(block_permutation, received, up, down)


def solution(mesh):
    return jax.shard_map(
        per_device,
        mesh=mesh,
        in_specs=(
            P(None, ("fsdp", "tp"), None),
            P(None, None, ("fsdp", "tp")),
            P(None, "fsdp", None),
            P(),
        ),
        out_specs=P(None, "fsdp", "tp"),
        check_vma=False,
    )
```

time: 149 us -> 146 us (0.980)
  blocking collectives: 120 us -> 117 us
    all_to_all x1, blocking collectives: 120 us -> 117 us  [exchange(): return lax.all_to_all(packed, 'tp', split_axis=0, concat_axis=0, tiled=True)]
  transfers between devices with their start and end apart: 1 -> 2, of which waited for: 0 -> 0; matrix products, arithmetic and copies ran while one was open for 0% -> 0% of each run, Pallas kernels for 4% -> 3%
where the time goes in v3:
time: 146 us
  blocking collectives  117 us (80%)
  Pallas kernels  14 us (10%)
  between operations  13.4 us (9%)
    all_to_all x1, blocking collectives, exchange(): return lax.all_to_all(packed, 'tp', split_axis=0, concat_axis=0, tiled=True)  117 us
    pallas_call x1, Pallas kernels, merge(): pl.pallas_call(kernel, out_shape=jax.ShapeDtypeStruct((layers, servers *...  9.24 us
    pallas_call x1, Pallas kernels, pack(): pl.pallas_call(kernel, out_shape=pltpu.VMEM((servers, chunk, rows, BLOCK)...  4.79 us
  transfers between devices with their start and end apart: 2, of which 0 were waited for; matrix products, arithmetic and copies ran while one was open for 0% of the time, Pallas kernels for 3%

profile of v3, /device:TPU:0, one launch (start us, length us, event | category | flops | bytes accessed | tf_op | source)
XLA Modules:
  0.0 145.6 jit_solution(16630334110351406130)
XLA Ops:
  6.5 0.0 all-gather.5.cloned.1.call-start
  6.5 0.7 all-gather.5.cloned.1.call-update
  7.3 0.0 all-gather.3.cloned.1.call-start
  7.3 0.7 all-gather.3.cloned.1.call-update
  8.0 121.5 %conditional.1 = (bf16[16,18,128,128]{3,2,1,0:T(8,128)(2,1)}) conditional(s32[]{:T(128)} %convert_element_type.3, () %tuple.11, (s32[144]{0:T(256)}, bf16[2,128,18432]{2,1,0:T(8,128)(2,1)}) %tuple.12), branch_computations={%region_0.0_spmd, %region_1.0_spmd} | conditional | bytes 18874376 | solution.py:159
  8.0 4.8 %pack.1 = bf16[16,18,128,128]{3,2,1,0:T(8,128)(2,1)S(1)} custom-call(s32[144]{0:T(256)} %get-tuple-element.12.order, bf16[2,128,18432]{2,1,0:T(8,128)(2,1)} %get-tuple-element.15.base), custom_call_target="tpu_custom_call" | custom-call | tf_op jit(solution)/shard_map/cond/branch_1_fun/pack/pallas_call | solution.py:41
  12.8 116.7 %all_to_all.4 = bf16[16,18,128,128]{3,2,1,0:T(8,128)(2,1)} all-to-all(bf16[16,18,128,128]{3,2,1,0:T(8,128)(2,1)S(1)} %pack.1), channel_id=1, replica_groups=mesh['fsdp'=8,'tp'=16] {'tp'}, dimensions={0} | all-to-all | bytes 18874368 | tf_op jit(solution)/shard_map/cond/branch_1_fun/all_to_all | solution.py:153
  129.5 0.0 all-gather.5.cloned.1.call-done
  129.5 0.0 all-gather.3.cloned.1.call-done.up
  129.5 9.2 %merge.1 = bf16[2,2048,1152]{2,1,0:T(8,128)(2,1)} custom-call(s32[144]{0:T(256)} %order.1, bf16[16,18,128,128]{3,2,1,0:T(8,128)(2,1)} %get-tuple-element.16.received, bf16[2,64,18432]{2,1,0:T(8,128)(2,1)} %all-gather.3.cloned.1.call-done.up, bf16[32,128,128]{2,1,0:T(8,128)(2,1)} %bitcast.2), custom_call_target="tpu_custom_call" | custom-call | tf_op jit(solution)/shard_map/merge/pallas_call | solution.py:112
Async XLA Ops:
  6.5 123.0 %all-gather.5.cloned.1.call-start = ((), (), s32[]{:S(2)}) async-start(), calls=%async_computation.2 | async-start | bytes 1081344 | tf_op jit(solution)/shard_map/all_gather | solution.py:143
  7.3 122.3 %all-gather.3.cloned.1.call-start = ((), (), s32[]{:S(2)}) async-start(), calls=%async_computation.1 | async-start | bytes 5308416 | tf_op jit(solution)/shard_map/all_gather | solution.py:139
Sparse Core Ops, SparseCore 0:
  9.7 64.1 all-gather.4
  75.5 35.8 all-gather.2

commit v4 on v3

--- a/solution.py
+++ b/solution.py
@@ -70,9 +70,9 @@
                 up_sem.at[0],
             ).start()
 
-        rank_rows = pl.ds(lax.axis_index("fsdp") % 2 * servers, servers)
-        load_down = pltpu.make_async_copy(downs.at[rank_rows], factor, down_sem.at[0])
-        load_down.start()
+        core = lax.axis_index("fsdp") % 2
+        for s in range(servers):
+            pltpu.make_async_copy(downs.at[2 * s + core], factor.at[s], down_sem.at[0]).start()
 
         def load(s):
             return pltpu.make_async_copy(received.at[s], held.at[s], load_sem.at[s])
@@ -80,7 +80,7 @@
         for s in range(servers):
             load(s).start()
         pltpu.make_async_copy(chosen, chosen, up_sem.at[0]).wait()
-        load_down.wait()
+        pltpu.make_async_copy(factor, factor, down_sem.at[0]).wait()
 
         @pl.loop(0, servers // SOURCES)
         def _(step):
@@ -145,7 +145,9 @@
         ("fsdp", "tp"),
         axis=0,
         tiled=True,
-        axis_index_groups=[[p * group + i for i in range(group)] for p in range(pairs)],
+        axis_index_groups=[
+            [(2 * p + core) * servers + t for t in range(servers) for core in range(2)] for p in range(pairs)
+        ],
     ).reshape(group, layers * ranks, rows)
 
     def exchange(order, base):

time: 146 us -> 145 us (level)
  no operation moved by 1% of the time
where the time goes in v4:
time: 145 us
  blocking collectives  117 us (81%)
  Pallas kernels  13.7 us (9%)
  between operations  13.4 us (9%)
    all_to_all x1, blocking collectives, exchange(): return lax.all_to_all(packed, 'tp', split_axis=0, concat_axis=0, tiled=True)  117 us
    pallas_call x1, Pallas kernels, merge(): pl.pallas_call(kernel, out_shape=jax.ShapeDtypeStruct((layers, servers *...  8.93 us
    pallas_call x1, Pallas kernels, pack(): pl.pallas_call(kernel, out_shape=pltpu.VMEM((servers, chunk, rows, BLOCK)...  4.79 us
  transfers between devices with their start and end apart: 2, of which 0 were waited for; matrix products, arithmetic and copies ran while one was open for 0% of the time, Pallas kernels for 3%

profile of v4, /device:TPU:0, one launch (start us, length us, event | category | flops | bytes accessed | tf_op | source)
XLA Modules:
  0.0 145.3 jit_solution(14885695131042322345)
XLA Ops:
  6.5 0.0 all-gather.5.cloned.1.call-start
  6.5 0.7 all-gather.5.cloned.1.call-update
  7.3 0.0 all-gather.3.cloned.1.call-start
  7.3 0.7 all-gather.3.cloned.1.call-update
  8.0 121.5 %conditional.1 = (bf16[16,18,128,128]{3,2,1,0:T(8,128)(2,1)}) conditional(s32[]{:T(128)} %convert_element_type.3, () %tuple.11, (s32[144]{0:T(256)}, bf16[2,128,18432]{2,1,0:T(8,128)(2,1)}) %tuple.12), branch_computations={%region_0.0_spmd, %region_1.0_spmd} | conditional | bytes 18874376 | solution.py:161
  8.0 4.8 %pack.1 = bf16[16,18,128,128]{3,2,1,0:T(8,128)(2,1)S(1)} custom-call(s32[144]{0:T(256)} %get-tuple-element.12.order, bf16[2,128,18432]{2,1,0:T(8,128)(2,1)} %get-tuple-element.15.base), custom_call_target="tpu_custom_call" | custom-call | tf_op jit(solution)/shard_map/cond/branch_1_fun/pack/pallas_call | solution.py:41
  12.8 116.7 %all_to_all.4 = bf16[16,18,128,128]{3,2,1,0:T(8,128)(2,1)} all-to-all(bf16[16,18,128,128]{3,2,1,0:T(8,128)(2,1)S(1)} %pack.1), channel_id=1, replica_groups=mesh['fsdp'=8,'tp'=16] {'tp'}, dimensions={0} | all-to-all | bytes 18874368 | tf_op jit(solution)/shard_map/cond/branch_1_fun/all_to_all | solution.py:155
  129.5 0.0 all-gather.5.cloned.1.call-done
  129.5 0.0 all-gather.3.cloned.1.call-done.up
  129.5 8.9 %merge.1 = bf16[2,2048,1152]{2,1,0:T(8,128)(2,1)} custom-call(s32[144]{0:T(256)} %order.1, bf16[16,18,128,128]{3,2,1,0:T(8,128)(2,1)} %get-tuple-element.16.received, bf16[2,64,18432]{2,1,0:T(8,128)(2,1)} %all-gather.3.cloned.1.call-done.up, bf16[32,128,128]{2,1,0:T(8,128)(2,1)} %bitcast.2), custom_call_target="tpu_custom_call" | custom-call | tf_op jit(solution)/shard_map/merge/pallas_call | solution.py:112
Async XLA Ops:
  6.5 123.0 %all-gather.5.cloned.1.call-start = ((), (), s32[]{:S(2)}) async-start(), calls=%async_computation.2 | async-start | bytes 1081344 | tf_op jit(solution)/shard_map/all_gather | solution.py:143
  7.3 122.3 %all-gather.3.cloned.1.call-start = ((), (), s32[]{:S(2)}) async-start(), calls=%async_computation.1 | async-start | bytes 5308416 | tf_op jit(solution)/shard_map/all_gather | solution.py:139
Sparse Core Ops, SparseCore 0:
  9.6 64.2 all-gather.4
  75.6 37.1 all-gather.2

commit v5 on v4

--- a/solution.py
+++ b/solution.py
@@ -104,8 +104,9 @@
                             part = delta[i * rows : (i + 1) * rows, j * BLOCK : (j + 1) * BLOCK]
                             at = pl.ds(pl.multiple_of(s * rows, rows), rows)
                             merged[layer, at, (c + j) * BLOCK : (c + j + 1) * BLOCK] = (base + part).astype(jnp.bfloat16)
-                at = pl.ds(pl.multiple_of(step * SOURCES * rows, rows), SOURCES * rows)
-                pltpu.make_async_copy(merged.at[layer, at], out.at[layer, at], store_sem.at[0]).start()
+                    at = pl.ds(pl.multiple_of(step * SOURCES * rows, rows), SOURCES * rows)
+                    cols = pl.ds(c * BLOCK, COLUMNS * BLOCK)
+                    pltpu.make_async_copy(merged.at[layer, at, cols], out.at[layer, at, cols], store_sem.at[0]).start()
 
         pltpu.make_async_copy(merged, out, store_sem.at[0]).wait()
 

time: 145 us -> 145 us (level)
  no operation moved by 1% of the time
where the time goes in v5:
time: 145 us
  blocking collectives  117 us (81%)
  Pallas kernels  13.5 us (9%)
  between operations  13.4 us (9%)
    all_to_all x1, blocking collectives, exchange(): return lax.all_to_all(packed, 'tp', split_axis=0, concat_axis=0, tiled=True)  117 us
    pallas_call x1, Pallas kernels, merge(): pl.pallas_call(kernel, out_shape=jax.ShapeDtypeStruct((layers, servers *...  8.68 us
    pallas_call x1, Pallas kernels, pack(): pl.pallas_call(kernel, out_shape=pltpu.VMEM((servers, chunk, rows, BLOCK)...  4.79 us
  transfers between devices with their start and end apart: 2, of which 0 were waited for; matrix products, arithmetic and copies ran while one was open for 0% of the time, Pallas kernels for 3%

profile of v5, /device:TPU:0, one launch (start us, length us, event | category | flops | bytes accessed | tf_op | source)
XLA Modules:
  0.0 145.0 jit_solution(14609631902402314432)
XLA Ops:
  6.5 0.0 all-gather.5.cloned.1.call-start
  6.5 0.7 all-gather.5.cloned.1.call-update
  7.3 0.0 all-gather.3.cloned.1.call-start
  7.3 0.7 all-gather.3.cloned.1.call-update
  8.0 121.5 %conditional.1 = (bf16[16,18,128,128]{3,2,1,0:T(8,128)(2,1)}) conditional(s32[]{:T(128)} %convert_element_type.3, () %tuple.11, (s32[144]{0:T(256)}, bf16[2,128,18432]{2,1,0:T(8,128)(2,1)}) %tuple.12), branch_computations={%region_0.0_spmd, %region_1.0_spmd} | conditional | bytes 18874376 | solution.py:162
  8.0 4.8 %pack.1 = bf16[16,18,128,128]{3,2,1,0:T(8,128)(2,1)S(1)} custom-call(s32[144]{0:T(256)} %get-tuple-element.12.order, bf16[2,128,18432]{2,1,0:T(8,128)(2,1)} %get-tuple-element.15.base), custom_call_target="tpu_custom_call" | custom-call | tf_op jit(solution)/shard_map/cond/branch_1_fun/pack/pallas_call | solution.py:41
  12.8 116.7 %all_to_all.4 = bf16[16,18,128,128]{3,2,1,0:T(8,128)(2,1)} all-to-all(bf16[16,18,128,128]{3,2,1,0:T(8,128)(2,1)S(1)} %pack.1), channel_id=1, replica_groups=mesh['fsdp'=8,'tp'=16] {'tp'}, dimensions={0} | all-to-all | bytes 18874368 | tf_op jit(solution)/shard_map/cond/branch_1_fun/all_to_all | solution.py:156
  129.5 0.0 all-gather.5.cloned.1.call-done
  129.5 0.0 all-gather.3.cloned.1.call-done.up
  129.5 8.7 %merge.1 = bf16[2,2048,1152]{2,1,0:T(8,128)(2,1)} custom-call(s32[144]{0:T(256)} %order.1, bf16[16,18,128,128]{3,2,1,0:T(8,128)(2,1)} %get-tuple-element.16.received, bf16[2,64,18432]{2,1,0:T(8,128)(2,1)} %all-gather.3.cloned.1.call-done.up, bf16[32,128,128]{2,1,0:T(8,128)(2,1)} %bitcast.2), custom_call_target="tpu_custom_call" | custom-call | tf_op jit(solution)/shard_map/merge/pallas_call | solution.py:113
Async XLA Ops:
  6.5 123.0 %all-gather.5.cloned.1.call-start = ((), (), s32[]{:S(2)}) async-start(), calls=%async_computation.2 | async-start | bytes 1081344 | tf_op jit(solution)/shard_map/all_gather | solution.py:144
  7.3 122.3 %all-gather.3.cloned.1.call-start = ((), (), s32[]{:S(2)}) async-start(), calls=%async_computation.1 | async-start | bytes 5308416 | tf_op jit(solution)/shard_map/all_gather | solution.py:140
Sparse Core Ops, SparseCore 0:
  9.6 64.2 all-gather.4
  75.6 37.1 all-gather.2

commit v6 on v5

--- a/solution.py
+++ b/solution.py
@@ -21,22 +21,26 @@
     chunk = layers * per_server
     stripes = rows // STRIPE
 
+    pieces = [(s // stripes, s % stripes * STRIPE, STRIPE) for s in range(layers * stripes)]
+    layer, row, size = pieces.pop()
+    pieces += [(layer, row, size // 2), (layer, row + size // 2, size // 2)]
+
     def kernel(order, base, packed, held, load_sem):
         def load(s):
-            return pltpu.make_async_copy(
-                base.at[s // stripes, pl.ds(s % stripes * STRIPE, STRIPE)], held.at[s], load_sem.at[s]
-            )
+            layer, row, size = pieces[s]
+            at = pl.ds(row, size)
+            return pltpu.make_async_copy(base.at[layer, at], held.at[layer, at], load_sem.at[s])
 
-        for s in range(layers * stripes):
+        for s in range(len(pieces)):
             load(s).start()
-        for s in range(layers * stripes):
-            layer, at = s // stripes, pl.ds(s % stripes * STRIPE, STRIPE)
+        for s, (layer, row, size) in enumerate(pieces):
+            at = pl.ds(row, size)
             load(s).wait()
 
             @pl.loop(0, servers, unroll=4)
             def _(d):
                 for c in range(per_server):
-                    packed[d, layer * per_server + c, at] = held[s, :, block_at(order, d * per_server + c)]
+                    packed[d, layer * per_server + c, at] = held[layer, at, block_at(order, d * per_server + c)]
 
     return pl.pallas_call(
         kernel,
@@ -47,8 +51,8 @@
         ],
         out_specs=pl.BlockSpec(memory_space=pltpu.VMEM),
         scratch_shapes=[
-            pltpu.VMEM((layers * stripes, STRIPE, columns), jnp.bfloat16),
-            pltpu.SemaphoreType.DMA((layers * stripes,)),
+            pltpu.VMEM((layers, rows, columns), jnp.bfloat16),
+            pltpu.SemaphoreType.DMA((len(pieces),)),
         ],
         compiler_params=pltpu.CompilerParams(vmem_limit_bytes=40 << 20),
         name="pack",

time: 145 us -> 145 us (level)
  no operation moved by 1% of the time
where the time goes in v6:
time: 145 us
  blocking collectives  117 us (81%)
  Pallas kernels  13.7 us (9%)
  between operations  13.4 us (9%)
    all_to_all x1, blocking collectives, exchange(): return lax.all_to_all(packed, 'tp', split_axis=0, concat_axis=0, tiled=True)  117 us
    pallas_call x1, Pallas kernels, merge(): pl.pallas_call(kernel, out_shape=jax.ShapeDtypeStruct((layers, servers *...  8.68 us
    pallas_call x1, Pallas kernels, pack(): pl.pallas_call(kernel, out_shape=pltpu.VMEM((servers, chunk, rows, BLOCK)...  4.98 us
  transfers between devices with their start and end apart: 2, of which 0 were waited for; matrix products, arithmetic and copies ran while one was open for 0% of the time, Pallas kernels for 3%

profile of v6, /device:TPU:0, one launch (start us, length us, event | category | flops | bytes accessed | tf_op | source)
XLA Modules:
  0.0 145.2 jit_solution(16676010910105861791)
XLA Ops:
  6.5 0.0 all-gather.5.cloned.1.call-start
  6.5 0.7 all-gather.5.cloned.1.call-update
  7.3 0.0 all-gather.3.cloned.1.call-start
  7.3 0.7 all-gather.3.cloned.1.call-update
  8.0 121.7 %conditional.1 = (bf16[16,18,128,128]{3,2,1,0:T(8,128)(2,1)}) conditional(s32[]{:T(128)} %convert_element_type.3, () %tuple.11, (s32[144]{0:T(256)}, bf16[2,128,18432]{2,1,0:T(8,128)(2,1)}) %tuple.12), branch_computations={%region_0.0_spmd, %region_1.0_spmd} | conditional | bytes 18874376 | solution.py:166
  8.0 5.0 %pack.1 = bf16[16,18,128,128]{3,2,1,0:T(8,128)(2,1)S(1)} custom-call(s32[144]{0:T(256)} %get-tuple-element.12.order, bf16[2,128,18432]{2,1,0:T(8,128)(2,1)} %get-tuple-element.15.base), custom_call_target="tpu_custom_call" | custom-call | tf_op jit(solution)/shard_map/cond/branch_1_fun/pack/pallas_call | solution.py:45
  13.0 116.7 %all_to_all.4 = bf16[16,18,128,128]{3,2,1,0:T(8,128)(2,1)} all-to-all(bf16[16,18,128,128]{3,2,1,0:T(8,128)(2,1)S(1)} %pack.1), channel_id=1, replica_groups=mesh['fsdp'=8,'tp'=16] {'tp'}, dimensions={0} | all-to-all | bytes 18874368 | tf_op jit(solution)/shard_map/cond/branch_1_fun/all_to_all | solution.py:160
  129.7 0.0 all-gather.5.cloned.1.call-done
  129.7 0.0 all-gather.3.cloned.1.call-done.up
  129.7 8.7 %merge.1 = bf16[2,2048,1152]{2,1,0:T(8,128)(2,1)} custom-call(s32[144]{0:T(256)} %order.1, bf16[16,18,128,128]{3,2,1,0:T(8,128)(2,1)} %get-tuple-element.16.received, bf16[2,64,18432]{2,1,0:T(8,128)(2,1)} %all-gather.3.cloned.1.call-done.up, bf16[32,128,128]{2,1,0:T(8,128)(2,1)} %bitcast.2), custom_call_target="tpu_custom_call" | custom-call | tf_op jit(solution)/shard_map/merge/pallas_call | solution.py:117
Async XLA Ops:
  6.5 123.2 %all-gather.5.cloned.1.call-start = ((), (), s32[]{:S(2)}) async-start(), calls=%async_computation.2 | async-start | bytes 1081344 | tf_op jit(solution)/shard_map/all_gather | solution.py:148
  7.3 122.4 %all-gather.3.cloned.1.call-start = ((), (), s32[]{:S(2)}) async-start(), calls=%async_computation.1 | async-start | bytes 5308416 | tf_op jit(solution)/shard_map/all_gather | solution.py:144
Sparse Core Ops, SparseCore 0:
  9.6 64.5 all-gather.4
  75.9 37.0 all-gather.2
